TPU v7x, 32 devices: a whole 2x2x4 slice. The times are simulated.
32 devices in a mesh: grp: 2 (over y), ctx: 8 (over z, x), head: 2 (over core).
Axes of the slice: x: 2, y: 2, z: 4, core: 2. Of those that a mesh axis runs over, the one named last changes fastest.
Arguments:
- query: bfloat16 [2048, 1024], P(('grp', 'ctx', 'head')), parts along dimension 0, may hold values from -6 to 6
- key: bfloat16 [2048, 1024], P(('grp', 'ctx', 'head')), parts along dimension 0, may hold values from -6 to 6
- value: bfloat16 [2048, 1024], P(('grp', 'ctx', 'head')), parts along dimension 0, may hold values from -6 to 6
- beta_logit: bfloat16 [2048, 8], P(('grp', 'ctx', 'head')), parts along dimension 0, may hold values from -10 to 11
- turn_ids: int32 [2048], P(('grp', 'ctx')), parts along dimension 0, may hold values from 0 to 3, never falling along the last dimension, each value on 1 to 512 neighbouring positions
- d_out: bfloat16 [2048, 1024], P(('grp', 'ctx', 'head')), parts along dimension 0, may hold values from -6 to 6
Outputs:
- out: bfloat16 [2048, 1024], P(('grp', 'ctx', 'head')), parts along dimension 0
- grad_query: bfloat16 [2048, 1024], P(('grp', 'ctx', 'head')), parts along dimension 0
- grad_key: bfloat16 [2048, 1024], P(('grp', 'ctx', 'head')), parts along dimension 0
- grad_value: bfloat16 [2048, 1024], P(('grp', 'ctx', 'head')), parts along dimension 0
- grad_beta: bfloat16 [2048, 8], P(('grp', 'ctx', 'head')), parts along dimension 0
There are 2 independent parts, one for each index of `grp`. A program takes and returns all parts, laid end to end along the dimension named above; each array names one. Nothing has to cross between parts.
Inputs may be any that keep to these rules, and one draw needn't show every extreme that they name: turn_ids never decrease along the tokens; equal ids form one turn block of at most 512 tokens.
All inputs are finite; a program needn't handle non-finite values.
Results may differ from a plain program's by a relative error of at most 0.0012.
Values may be sent and summed in bfloat16 or wider, within the bound.
A program may use at most 256 MiB of HBM per device.

v0:
```python
import jax
import jax.numpy as jnp
from jax import lax
from jax.sharding import PartitionSpec as P

HEAD_COUNT = 8
DK = 128
BLOCK = 64


highest = lax.Precision.HIGHEST
epsilon = 1e-06


def shifted(value, axis, steps):
    count = lax.axis_size(axis)
    leading, last = (max(0, -steps), min(count, count - steps))
    return lax.ppermute(value, axis, [(source, source + steps) for source in range(leading, last)])


def carried_in(shard, axis, combine, identity, reverse):
    size, index = (lax.axis_size(axis), lax.axis_index(axis))
    everything = jax.tree.map(lambda part: lax.all_gather(part, axis), shard)
    start = jax.tree.map(
        lambda part, zero: jnp.broadcast_to(jnp.asarray(zero, part.dtype), part.shape),
        shard,
        identity,
    )

    def turn(k, before):
        at = size - 1 - k if reverse else k
        reached = at > index if reverse else at < index
        new = combine(before, jax.tree.map(lambda part: part[at], everything))
        return jax.tree.map(lambda a, b: jnp.where(reached, a, b), new, before)

    return lax.fori_loop(0, size, turn, start)


def unit_rows(vectors):
    return vectors / jnp.sqrt(jnp.sum(vectors * vectors, axis=-1, keepdims=True) + epsilon)


def block_masks(turn_block, before):
    length = turn_block.shape[0]
    row_index = lax.broadcasted_iota(jnp.int32, (length, length), 0)
    col_index = lax.broadcasted_iota(jnp.int32, (length, length), 1)
    same_turn = turn_block[:, None] == turn_block[None, :]
    strict = jnp.where(same_turn & (row_index > col_index), 1.0, 0.0).astype(jnp.float32)
    inclusive = jnp.where(same_turn & (row_index >= col_index), 1.0, 0.0).astype(jnp.float32)
    continues = jnp.where(turn_block == before, 1.0, 0.0).astype(jnp.float32)
    in_last = jnp.where(turn_block == turn_block[length - 1], 1.0, 0.0).astype(jnp.float32)
    return (strict, inclusive, continues, in_last)


def block_state(state, keys, values, rates, turn_block, before):
    strict, inclusive, continues, in_last = block_masks(turn_block, before)
    length = keys.shape[0]
    key_gram = jnp.einsum("ihd,jhd->hij", keys, keys, precision=highest)
    scaled = jnp.transpose(rates)[:, :, None]
    system = jnp.eye(length, dtype=keys.dtype)[None] + scaled * key_gram * strict[None]
    predicted = jnp.einsum("ihd,hde->hie", keys, state, precision=highest)
    targets = scaled * (jnp.transpose(values, (1, 0, 2)) - continues[None, :, None] * predicted)
    updates = lax.linalg.triangular_solve(system, targets, left_side=True, lower=True)
    new_state = continues[length - 1] * state + jnp.einsum(
        "ihd,hie->hde", keys, in_last[None, :, None] * updates, precision=highest
    )
    return (new_state, updates)


def block_output(state, queries, keys, updates, turn_block, before):
    strict, inclusive, continues, in_last = block_masks(turn_block, before)
    scores = jnp.einsum("ihd,jhd->hij", queries, keys, precision=highest) * inclusive[None]
    carried = (
        jnp.einsum("ihd,hde->ihe", queries, state, precision=highest) * continues[:, None, None]
    )
    within = jnp.einsum("hij,hje->ihe", scores, updates, precision=highest)
    return carried + within


def block_befores(turn_ids, first_before):
    blocks = turn_ids.shape[0] // BLOCK
    turn_blocks = turn_ids.reshape(blocks, BLOCK)
    first = jnp.reshape(jnp.asarray(first_before), (1,))
    befores = jnp.concatenate([first, turn_blocks[:-1, BLOCK - 1]])
    return (turn_blocks, befores)


def run_layer(query, key, value, beta_logit, turn_ids, first_before, start_state):
    tokens = query.shape[0]
    heads = beta_logit.shape[1]
    width = query.shape[1] // heads
    blocks = tokens // BLOCK
    queries = unit_rows(query.astype(jnp.float32).reshape(tokens, heads, width))
    keys = unit_rows(key.astype(jnp.float32).reshape(tokens, heads, width))
    values = value.astype(jnp.float32).reshape(tokens, heads, width)
    rates = 2.0 * jax.nn.sigmoid(beta_logit.astype(jnp.float32))
    turn_blocks, befores = block_befores(turn_ids, first_before)

    def run_advance(state, inputs_block):
        query_block, key_block, value_block, rate_block, turn_block, before = inputs_block
        new_state, updates = block_state(
            state, key_block, value_block, rate_block, turn_block, before
        )
        outputs = block_output(state, query_block, key_block, updates, turn_block, before)
        return (new_state, outputs)

    final_state, outputs = lax.scan(
        jax.checkpoint(run_advance),
        start_state,
        (
            queries.reshape(blocks, BLOCK, heads, width),
            keys.reshape(blocks, BLOCK, heads, width),
            values.reshape(blocks, BLOCK, heads, width),
            rates.reshape(blocks, BLOCK, heads),
            turn_blocks,
            befores,
        ),
    )
    return (outputs.reshape(tokens, heads * width), final_state)


def transitions(unit_keys, values, rates, turn_blocks, befores):
    tokens, heads, width = unit_keys.shape
    blocks = tokens // BLOCK
    unit_matrix = jnp.broadcast_to(jnp.eye(width, dtype=jnp.float32), (heads, width, width))
    start_state = jnp.concatenate([unit_matrix, jnp.zeros_like(unit_matrix)], axis=2)
    pair_values = jnp.concatenate([jnp.zeros_like(values), values], axis=2)

    def transitions_advance(state, inputs_block):
        key_block, value_block, rate_block, turn_block, before = inputs_block
        new_state, updates = block_state(
            state, key_block, value_block, rate_block, turn_block, before
        )
        return (new_state, (state, updates))

    final_state, stored = lax.scan(
        transitions_advance,
        start_state,
        (
            unit_keys.reshape(blocks, BLOCK, heads, width),
            pair_values.reshape(blocks, BLOCK, heads, 2 * width),
            rates.reshape(blocks, BLOCK, heads),
            turn_blocks,
            befores,
        ),
    )
    return (final_state, stored[0], stored[1])


def compose(earlier, later):
    joined = jnp.einsum("hij,hjk->hik", later[0], earlier[0], precision=highest)
    offset = jnp.einsum("hij,hjk->hik", later[0], earlier[1], precision=highest) + later[1]
    return (joined, offset)


def on_device(query, key, value, beta_logit, turn_ids, d_out):
    share = HEAD_COUNT // lax.axis_size("head")
    width = DK
    moved = shifted(turn_ids[-1:] + 1, "ctx", 1)
    first_before = moved[0] - 1
    queries, keys, values, logits, upstream = (
        lax.all_to_all(query, "head", split_axis=1, concat_axis=0, tiled=True),
        lax.all_to_all(key, "head", split_axis=1, concat_axis=0, tiled=True),
        lax.all_to_all(value, "head", split_axis=1, concat_axis=0, tiled=True),
        lax.all_to_all(beta_logit, "head", split_axis=1, concat_axis=0, tiled=True),
        lax.all_to_all(d_out, "head", split_axis=1, concat_axis=0, tiled=True),
    )
    tokens = keys.shape[0]
    blocks = tokens // BLOCK
    turn_blocks, befores = block_befores(turn_ids, first_before)
    unit_keys = unit_rows(keys.astype(jnp.float32).reshape(tokens, share, width))
    rates = 2.0 * jax.nn.sigmoid(logits.astype(jnp.float32))
    final_state, starts, updates = transitions(
        unit_keys,
        values.astype(jnp.float32).reshape(tokens, share, width),
        rates,
        turn_blocks,
        befores,
    )
    unit_matrix = jnp.broadcast_to(jnp.eye(width, dtype=jnp.float32), (share, width, width))
    empty = jnp.zeros((share, width, width), jnp.float32)
    transfer = final_state[:, :, :width]
    prefix = carried_in(
        (transfer, final_state[:, :, width:]), "ctx", compose, (unit_matrix, empty), False
    )
    state_in = prefix[1]
    unit_queries = unit_rows(queries.astype(jnp.float32).reshape(tokens, share, width))
    query_blocks = unit_queries.reshape(blocks, BLOCK, share, width)
    key_blocks = unit_keys.reshape(blocks, BLOCK, share, width)
    through = jax.vmap(block_output)(
        starts[..., :width], query_blocks, key_blocks, updates[..., :width], turn_blocks, befores
    ).reshape(tokens, share, width)
    upstream_full = upstream.astype(jnp.float32)
    response = jnp.einsum(
        "thd,the->hde", through, upstream_full.reshape(tokens, share, width), precision=highest
    )
    carried_back = carried_in(
        (jnp.swapaxes(transfer, 1, 2), response), "ctx", compose, (unit_matrix, empty), True
    )

    def local_layer(first_arg, second_arg, third_arg, fourth_arg, fifth_arg):
        return run_layer(
            first_arg, second_arg, third_arg, fourth_arg, turn_ids, first_before, fifth_arg
        )

    primal, pullback = jax.vjp(local_layer, queries, keys, values, logits, state_in)
    gradients = pullback((upstream_full, carried_back[1]))
    grad_parts = (gradients[0], gradients[1], gradients[2], gradients[3])
    returned = (
        lax.all_to_all(
            primal[0].astype(jnp.bfloat16), "head", split_axis=0, concat_axis=1, tiled=True
        ),
        lax.all_to_all(grad_parts[0], "head", split_axis=0, concat_axis=1, tiled=True),
        lax.all_to_all(grad_parts[1], "head", split_axis=0, concat_axis=1, tiled=True),
        lax.all_to_all(grad_parts[2], "head", split_axis=0, concat_axis=1, tiled=True),
        lax.all_to_all(grad_parts[3], "head", split_axis=0, concat_axis=1, tiled=True),
    )
    return (returned[0], returned[1], returned[2], returned[3], returned[4])


def solution(mesh):
    return jax.shard_map(
        on_device,
        mesh=mesh,
        in_specs=(
            P(("grp", "ctx", "head"), None),
            P(("grp", "ctx", "head"), None),
            P(("grp", "ctx", "head"), None),
            P(("grp", "ctx", "head"), None),
            P(("grp", "ctx")),
            P(("grp", "ctx", "head"), None),
        ),
        out_specs=(
            P(("grp", "ctx", "head"), None),
            P(("grp", "ctx", "head"), None),
            P(("grp", "ctx", "head"), None),
            P(("grp", "ctx", "head"), None),
            P(("grp", "ctx", "head"), None),
        ),
        check_vma=False,
    )
```

profile of v0, /device:TPU:0, one launch (start us, length us, event | category | flops | bytes accessed | tf_op | source)
XLA Modules:
  0.0 465.9 jit_solution(186789755569948464)
XLA Ops:
  8.7 3.4 all-to-all-start
  14.0 6.1 %collective-permute-start = (s32[1]{0:T(128)}, s32[1]{0:T(128)}, u32[]{:S(2)}, u32[]{:S(2)}) collective-permute-start(s32[1]{0:T(128)} %add.222), channel_id=1, source_target_pairs={{0,2},{2,4},{4,6},{6,8},{8,10},{10,12},{12,14},{1,3},{3,5},{5,7},{... | collective-permute-start | bytes 20 | tf_op jit(solution)/shard_map/ppermute | solution.py:18
  22.5 3.4 all-to-all-start.3
  33.5 3.4 all-to-all-start.2
  38.4 3.4 all-to-all-start.5
  45.3 51.2 %while.83 = (s32[]{:T(128)}, f32[4,128,256]{2,1,0:T(8,128)S(1)}, f32[2,4,128,256]{3,2,1,0:T(8,128)}, f32[2,4,64,256]{3,2,1,0:T(8,128)S(1)}, s32[2,64]{1,0:T(2,12...) while((s32[]{:T(128)}, f32[4,128,256]{2,1,0:T(8,128)S(1)}, ...), condition=%wide.region_2.3_spmd, body=%wide.region_1.2_spmd.sunk | while | flops 277442816 | bytes 13293277 | solution.py:136
  47.0 19.7 %custom-call.28 = f32[4,1,64,64]{2,3,1,0:T(8,128)S(1)} custom-call(f32[4,1,64,64]{3,2,1,0:T(8,128)S(1)} %fusion.264), custom_call_target="InvertDiagBlocksLowerTriangular" | custom-call | tf_op jit(solution)/shard_map/while/body/eval_jaxpr/triangular_solve | solution.py:63
  72.6 19.7 %custom-call.28 = f32[4,1,64,64]{2,3,1,0:T(8,128)S(1)} custom-call(f32[4,1,64,64]{3,2,1,0:T(8,128)S(1)} %fusion.264), custom_call_target="InvertDiagBlocksLowerTriangular" | custom-call | tf_op jit(solution)/shard_map/while/body/eval_jaxpr/triangular_solve | solution.py:63
  106.8 42.7 %all-gather.15.cloned.1.call-done = f32[32,128,128]{2,1,0:T(8,128)} async-done(((f32[4,128,128]{2,1,0:T(8,128)}), f32[32,128,128]{2,1,0:T(8,128)}) %all-gather.15.cloned.1.call-update) | async-done | bytes 2097168 | tf_op jit(solution)/shard_map/all_gather | solution.py:23
  149.5 49.9 %all-gather.13.cloned.1.call-done = f32[32,128,128]{2,1,0:T(8,128)} async-done(((f32[4,128,128]{2,1,0:T(8,128)}), f32[32,128,128]{2,1,0:T(8,128)}) %all-gather.13.cloned.1.call-update) | async-done | bytes 2097168 | tf_op jit(solution)/shard_map/all_gather | solution.py:23
  199.4 11.9 %while.87 = (s32[]{:T(128)}, f32[4,128,128]{2,1,0:T(8,128)S(1)}, s32[]{:T(128)}, f32[8,4,128,128]{3,2,1,0:T(8,128)}, f32[8,4,128,128]{3,2,1,0:T(8,128)}, /*index=5*/s32[]{:T(128)}, s32[]{:T(128)}, s32[]{:T(128)}, s32[]{:T(128)}) while((s32[]{:T(128)}, f32[4,128,128]{2,1,0:T(8,128)S(1)}, s32[]{:T(128)}, ...), condition=%wide.region_9.11_spmd.clone, body=%wide.region_8.10_spmd.clone.sunk | while | flops 100925448 | bytes 1837725 | solution.py:36
  211.4 38.0 %all-gather.9.cloned.1.call-done = f32[32,128,128]{2,1,0:T(8,128)} async-done(((f32[4,128,128]{2,1,0:T(8,128)}), f32[32,128,128]{2,1,0:T(8,128)}) %all-gather.9.cloned.1.call-update) | async-done | bytes 2097168 | tf_op jit(solution)/shard_map/all_gather | solution.py:23
  249.4 49.8 %all-gather.11.cloned.1.call-done = f32[32,128,128]{2,1,0:T(8,128)} async-done(((f32[4,128,128]{2,1,0:T(8,128)}), f32[32,128,128]{2,1,0:T(8,128)}) %all-gather.11.cloned.1.call-update) | async-done | bytes 2097168 | tf_op jit(solution)/shard_map/all_gather | solution.py:23
  299.2 11.8 %while.86 = (s32[]{:T(128)}, f32[4,128,128]{2,1,0:T(8,128)S(1)}, s32[]{:T(128)}, f32[8,4,128,128]{3,2,1,0:T(8,128)}, f32[8,4,128,128]{3,2,1,0:T(8,128)}, /*index=5*/s32[]{:T(128)}, s32[]{:T(128)}) while((s32[]{:T(128)}, f32[4,128,128]{2,1,0:T(8,128)S(1)}, s32[]{:T(128)}, f32[8,4,128,128]{3,2,1,0:T(8,128)}, ...), condition=%wide.region_4.5_spmd.clone, body=%wide.region_3.4_spmd.clone.sunk | while | flops 100925440 | bytes 1837663 | solution.py:36
  311.1 52.7 %while.85 = (s32[]{:T(128)}, f32[4,128,128]{2,1,0:T(8,128)S(1)}, bf16[2,64,4,128]{3,1,2,0:T(8,128)(2,1)S(1)}, f32[2,4,128,128]{3,2,1,0:T(8,128)S(1)}, s32[2,64]{...) while((s32[]{:T(128)}, f32[4,128,128]{2,1,0:T(8,128)S(1)}, ...), condition=%wide.region_7.9_spmd.clone, body=%wide.region_6.8_spmd.clone.sunk | while | flops 252109056 | bytes 3973289 | solution.py:107
  312.8 19.7 %custom-call.30 = f32[4,1,64,64]{2,3,1,0:T(8,128)S(1)} custom-call(f32[4,1,64,64]{3,2,1,0:T(8,128)S(1)} %fusion.328), custom_call_target="InvertDiagBlocksLowerTriangular" | custom-call | tf_op jit(solution)/shard_map/jvp()/while/body/eval_jaxpr/triangular_solve/custom-call.0 | solution.py:63
  339.2 19.7 %custom-call.30 = f32[4,1,64,64]{2,3,1,0:T(8,128)S(1)} custom-call(f32[4,1,64,64]{3,2,1,0:T(8,128)S(1)} %fusion.328), custom_call_target="InvertDiagBlocksLowerTriangular" | custom-call | tf_op jit(solution)/shard_map/jvp()/while/body/eval_jaxpr/triangular_solve/custom-call.0 | solution.py:63
  365.3 66.6 %while.84 = (s32[]{:T(128)}, f32[4,128,128]{2,1,0:T(8,128)S(1)}, f32[2,64,4,128]{3,2,1,0:T(4,128)S(1)}, f32[2,64,4,128]{3,2,1,0:T(4,128)}, bf16[2,64,4,128]{3,1,...) while((s32[]{:T(128)}, f32[4,128,128]{2,1,0:T(8,128)S(1)}, ...), condition=%wide.region_13.15_spmd, body=%wide.region_10.14_spmd.sunk | while | flops 642899968 | bytes 13992481 | solution.py:107
  369.6 19.7 %custom-call.29 = f32[4,1,64,64]{2,3,1,0:T(8,128)S(1)} custom-call(f32[4,1,64,64]{3,2,1,0:T(8,128)S(1)} %select_bitcast_fusion.2), custom_call_target="InvertDiagBlocksLowerTriangular" | custom-call | tf_op jit(solution)/shard_map/transpose(jvp())/while/body/eval_jaxpr/checkpoint/triangular_solve | solution.py:63
  402.9 19.7 %custom-call.29 = f32[4,1,64,64]{2,3,1,0:T(8,128)S(1)} custom-call(f32[4,1,64,64]{3,2,1,0:T(8,128)S(1)} %select_bitcast_fusion.2), custom_call_target="InvertDiagBlocksLowerTriangular" | custom-call | tf_op jit(solution)/shard_map/transpose(jvp())/while/body/eval_jaxpr/checkpoint/triangular_solve | solution.py:63
  435.1 3.8 all_to_all.148
  440.7 3.8 all_to_all.149
  445.3 3.8 all_to_all.150
  450.5 3.8 all_to_all.151
  (333 shorter events, 115.2 us)
Async XLA Ops:
  7.2 19.4 %copy-start.19 = (bf16[64,8]{0,1:T(8,128)(2,1)S(1)}, bf16[64,8]{0,1:T(8,128)(2,1)}, u32[]{:S(2)}) copy-start(bf16[64,8]{0,1:T(8,128)(2,1)} %param.21) | copy-start | bytes 3076
  8.7 13.8 %all-to-all-start = ((bf16[64,2,512]{2,0,1:T(8,128)(2,1)}), bf16[64,2,512]{2,0,1:T(8,128)(2,1)S(1)}, u32[]{:S(2)}, u32[]{:S(2)}) async-start(bf16[64,2,512]{2,0,1:T(8,128)(2,1)} %bitcast.312), calls=%async_computation | async-start | bytes 262144 | tf_op jit(solution)/shard_map/all_to_all | solution.py:163
  14.0 29.8 %collective-permute-start = (s32[1]{0:T(128)}, s32[1]{0:T(128)}, u32[]{:S(2)}, u32[]{:S(2)}) collective-permute-start(s32[1]{0:T(128)} %add.222), channel_id=1, source_target_pairs={{0,2},{2,4},{4,6},{6,8},{8,10},{10,12},{12,14},{1,3},{3,5},{5,7},{... | collective-permute-start | bytes 20 | tf_op jit(solution)/shard_map/ppermute | solution.py:18
  22.5 8.8 %copy-start.7 = (bf16[64,2,512]{2,0,1:T(8,128)(2,1)}, bf16[64,2,512]{2,0,1:T(8,128)(2,1)S(1)}, u32[]{:S(2)}) copy-start(bf16[64,2,512]{2,0,1:T(8,128)(2,1)S(1)} %all-to-all-done) | copy-start | bytes 393220
  22.5 4.8 %all-to-all-start.3 = ((bf16[64,2,512]{2,0,1:T(8,128)(2,1)}), bf16[64,2,512]{2,0,1:T(8,128)(2,1)S(1)}, u32[]{:S(2)}, u32[]{:S(2)}) async-start(bf16[64,2,512]{2,0,1:T(8,128)(2,1)} %bitcast.310), calls=%async_computation.3 | async-start | bytes 262144 | tf_op jit(solution)/shard_map/all_to_all | solution.py:162
  27.3 4.0 copy-start.5
  27.3 6.2 %all-to-all-start.1 = ((bf16[2,2,128]{2,1,0:T(2,128)(2,1)}), bf16[2,2,128]{2,1,0:T(2,128)(2,1)S(1)}, u32[]{:S(2)}, u32[]{:S(2)}) async-start(bf16[2,2,128]{2,1,0:T(2,128)(2,1)} %reshape.574), calls=%async_computation.1 | async-start | bytes 2048 | tf_op jit(solution)/shard_map/all_to_all | solution.py:165
  31.0 6.1 %copy-start.18 = (bf16[64,1024]{1,0:T(8,128)(2,1)S(1)}, bf16[64,1024]{1,0:T(8,128)(2,1)}, u32[]{:S(2)}) copy-start(bf16[64,1024]{1,0:T(8,128)(2,1)} %param.23) | copy-start | bytes 393220
  31.3 10.5 %copy-start.4 = (f32[2,64,4,128]{3,2,1,0:T(4,128)}, f32[2,64,4,128]{3,2,1,0:T(4,128)S(1)}, u32[]{:S(2)}) copy-start(f32[2,64,4,128]{3,2,1,0:T(4,128)S(1)} %reshape.560) | copy-start | bytes 786436
  33.5 4.8 %all-to-all-start.2 = ((bf16[64,2,512]{2,0,1:T(8,128)(2,1)}), bf16[64,2,512]{2,0,1:T(8,128)(2,1)S(1)}, u32[]{:S(2)}, u32[]{:S(2)}) async-start(bf16[64,2,512]{2,0,1:T(8,128)(2,1)} %bitcast.311), calls=%async_computation.2 | async-start | bytes 262144 | tf_op jit(solution)/shard_map/all_to_all | solution.py:164
  38.4 4.8 %all-to-all-start.5 = ((bf16[64,2,512]{2,0,1:T(8,128)(2,1)}), bf16[64,2,512]{2,0,1:T(8,128)(2,1)S(1)}, u32[]{:S(2)}, u32[]{:S(2)}) async-start(bf16[64,2,512]{2,0,1:T(8,128)(2,1)} %bitcast.309), calls=%async_computation.5 | async-start | bytes 262144 | tf_op jit(solution)/shard_map/all_to_all | solution.py:166
  41.7 107.7 %all-gather.15.cloned.1.call-start = ((), (), s32[]{:S(2)}) async-start(), calls=%async_computation.13 | async-start | bytes 2359296 | tf_op jit(solution)/shard_map/all_gather | solution.py:23
  99.7 99.7 %all-gather.13.cloned.1.call-start = ((), (), s32[]{:S(2)}) async-start(), calls=%async_computation.12 | async-start | bytes 2359296 | tf_op jit(solution)/shard_map/all_gather | solution.py:23
  101.5 147.9 %all-gather.9.cloned.1.call-start = ((), (), s32[]{:S(2)}) async-start(), calls=%async_computation.10 | async-start | bytes 2359296 | tf_op jit(solution)/shard_map/all_gather | solution.py:23
  102.2 196.9 %all-gather.11.cloned.1.call-start = ((), (), s32[]{:S(2)}) async-start(), calls=%async_computation.11 | async-start | bytes 2359296 | tf_op jit(solution)/shard_map/all_gather | solution.py:23
  392.0 3.8 copy-start
  425.2 3.8 copy-start
  431.8 7.8 %copy-start.3 = (f32[2,64,4,128]{3,2,1,0:T(4,128)S(1)}, f32[2,64,4,128]{3,2,1,0:T(4,128)}, u32[]{:S(2)}) copy-start(f32[2,64,4,128]{3,2,1,0:T(4,128)} %copy-done.2) | copy-start | bytes 786436
  431.8 7.8 %copy-start.16 = (f32[2,64,4]{2,1,0:T(8,128)S(1)}, f32[2,64,4]{2,1,0:T(8,128)}, u32[]{:S(2)}) copy-start(f32[2,64,4]{2,1,0:T(8,128)} %copy.230) | copy-start | bytes 6148
  434.8 5.8 %copy-start.6 = (bf16[64,2,512]{2,0,1:T(8,128)(2,1)S(1)}, bf16[64,2,512]{2,0,1:T(8,128)(2,1)}, u32[]{:S(2)}) copy-start(bf16[64,2,512]{2,0,1:T(8,128)(2,1)} %copy-done.5) | copy-start | bytes 393220
  434.8 5.8 %copy-start.9 = (f32[2,64,512]{2,1,0:T(8,128)S(1)}, f32[2,64,512]{2,1,0:T(8,128)}, u32[]{:S(2)}) copy-start(f32[2,64,512]{2,1,0:T(8,128)} %div.90) | copy-start | bytes 786436
  438.9 6.3 %copy-start.11 = (bf16[2,64,4,128]{3,1,2,0:T(8,128)(2,1)S(1)}, bf16[2,64,4,128]{3,1,2,0:T(8,128)(2,1)}, u32[]{:S(2)}) copy-start(bf16[2,64,4,128]{3,1,2,0:T(8,128)(2,1)} %get-tuple-element.761) | copy-start | bytes 393220
  439.7 10.7 %copy-start.13 = (bf16[2,64,4,128]{3,1,2,0:T(8,128)(2,1)S(1)}, bf16[2,64,4,128]{3,1,2,0:T(8,128)(2,1)}, u32[]{:S(2)}) copy-start(bf16[2,64,4,128]{3,1,2,0:T(8,128)(2,1)} %copy-done.12) | copy-start | bytes 393220
  454.3 4.4 all-to-all-start.9
  (11 other events, 24.1 us)
Sparse Core Ops, SparseCore 0:
  99.8 49.6 all-gather.14
  151.6 47.7 all-gather.12
  201.5 47.7 all-gather.8
  251.4 47.7 all-gather.10
where the time goes:
time: 467 us; the launch traced here: 466 us
  waiting for transfers between devices  184 us (39%)
  other arithmetic  131 us (28%)
  matrix products  57.8 us (12%)
  local copies, waits for them, and re-layouts  34.3 us (7%)
  starting transfers between devices  26.2 us (6%)
  between operations  15.7 us (3%)
  blocking collectives  15.4 us (3%)
    all_gather x4, waiting for transfers between devices, carried_in(): everything = jax.tree.map(lambda part: lax.all_gather(part, axis), shard)  180 us
    another operation x14, other arithmetic, block_state(): lax.linalg.triangular_solve(system, targets, left_side=True, lower=True)  118 us
    dot_general x16, matrix products, compose(): jnp.einsum('hij,hjk->hik', later[0], earlier[1], precision=highest)  22.9 us
  transfers between devices with their start and end apart: 11, of which 8 were waited for; matrix products, arithmetic and copies ran while one was open for 6% of the time, Pallas kernels for 0%

commit v1 on v0

v1 whole, which is shorter than its diff:
```python
import functools

import jax
import jax.numpy as jnp
from jax import lax
from jax.experimental import pallas as pl
from jax.experimental.pallas import tpu as pltpu
from jax.sharding import PartitionSpec as P

HEAD_COUNT = 8
DK = 128
epsilon = 1e-06
MESH = pl.DeviceIdType.MESH
f32 = jnp.float32
bf16 = jnp.bfloat16

NN = (((1,), (0,)), ((), ()))
NT = (((1,), (1,)), ((), ()))
TN = (((0,), (0,)), ((), ()))


def split(x):
    if x.dtype == bf16:
        return (x, None)
    high = x.astype(bf16)
    return (high, (x - high.astype(f32)).astype(bf16))


def product(a, b, dims=NN):
    left, right = [a[0]], [b[0]]
    if a[1] is not None:
        left.append(a[1])
        right.append(b[0])
    if b[1] is not None:
        left.append(a[0])
        right.append(b[1])
    (ca,), (cb,) = dims[0]
    left = jnp.concatenate(left, axis=ca) if len(left) > 1 else left[0]
    right = jnp.concatenate(right, axis=cb) if len(right) > 1 else right[0]
    return lax.dot_general(left, right, dims, preferred_element_type=f32)


def stack(a, b, axis=0):
    low = None
    if a[1] is not None or b[1] is not None:
        zero_a = jnp.zeros_like(a[0]) if a[1] is None else a[1]
        zero_b = jnp.zeros_like(b[0]) if b[1] is None else b[1]
        low = jnp.concatenate([zero_a, zero_b], axis=axis)
    return (jnp.concatenate([a[0], b[0]], axis=axis), low)


def unit(x):
    scale = lax.rsqrt(jnp.sum(x * x, axis=1, keepdims=True) + epsilon)
    return x * scale, scale


def column(row):
    return jnp.transpose(jnp.broadcast_to(row, (row.shape[1], row.shape[1])))


def kernel(
    groups, sub, ids_ref, logit_ref, q_ref, k_ref, v_ref, d_ref,
    out_ref, gq_ref, gk_ref, gv_ref, gb_ref,
    small_src, small, kb, vb, qb, db, yb, gqb, gkb, gvb, rate_src, rate_in,
    ahead_src, ahead, back_src, back,
    send_in, recv_in, send_out, recv_out, send_state, recv_state, local_sem,
):
    count = HEAD_COUNT
    cores = count // sub
    tokens = q_ref.shape[0]
    chunk = tokens * cores
    ctx, core = lax.axis_index("ctx"), lax.axis_index("head")
    group = ctx // sub
    me = (ctx % sub) * cores + core

    def device(member):
        return {"ctx": group * sub + member // cores, "head": member % cores}

    def others():
        return [lax.rem(me + d, count) for d in range(1, count)]

    def columns(member):
        return pl.ds(pl.multiple_of(member * DK, DK), DK)

    def rows(member):
        return pl.ds(pl.multiple_of(member * tokens, tokens), tokens)

    barrier = pltpu.get_barrier_semaphore()
    for other in others():
        pl.semaphore_signal(barrier, inc=1, device_id=device(other), device_id_type=MESH)
    waits = count - 1
    if groups > 1:
        @pl.when(group > 0)
        def _():
            pl.semaphore_signal(barrier, inc=1, device_id={"ctx": ctx - sub}, device_id_type=MESH)

        @pl.when(group < groups - 1)
        def _():
            pl.semaphore_signal(barrier, inc=1, device_id={"ctx": ctx + sub}, device_id_type=MESH)

        waits = waits + (group + groups - 1) // groups + (groups - 1 - group + groups - 1) // groups

    arrays = [(k_ref, kb), (v_ref, vb), (q_ref, qb), (d_ref, db)]
    own = [
        pltpu.make_async_copy(src.at[:, columns(me)], dst.at[rows(me), :], local_sem.at[i])
        for i, (src, dst) in enumerate(arrays)
    ]
    for copy in own:
        copy.start()

    logits = jnp.pad(logit_ref[...].astype(f32), ((0, 0), (0, DK - count)))
    placed = jnp.concatenate([jnp.where(core == c, logits, 0.0) for c in range(cores)], axis=0)
    small_src[0:8, :] = jnp.transpose(placed)[0:8, :]
    small_src[8:16, :] = jnp.broadcast_to(ids_ref[...].astype(f32), (8, chunk))
    small[me] = small_src[...]

    pl.semaphore_wait(barrier, waits)

    def copy_small(other, source):
        return pltpu.make_async_remote_copy(
            src_ref=small_src, dst_ref=small.at[source], send_sem=send_in.at[4, other],
            recv_sem=recv_in.at[4, source], device_id=device(other), device_id_type=MESH)

    def copy_in(i, other, source):
        src, dst = arrays[i]
        return pltpu.make_async_remote_copy(
            src_ref=src.at[:, columns(other)], dst_ref=dst.at[rows(source), :], send_sem=send_in.at[i, other],
            recv_sem=recv_in.at[i, source], device_id=device(other), device_id_type=MESH)

    for other in others():
        copy_in(0, other, me).start()
    for other in others():
        copy_small(other, me).start()
    for i in (1, 2, 3):
        for other in others():
            copy_in(i, other, me).start()

    def arrived(i):
        own[i].wait()
        for other in others():
            copy_in(i, other, other).wait_recv()

    row_index = lax.broadcasted_iota(jnp.int32, (chunk, chunk), 0)
    col_index = lax.broadcasted_iota(jnp.int32, (chunk, chunk), 1)
    eye = jnp.where(row_index == col_index, 1.0, 0.0).astype(f32)
    lower = row_index > col_index
    lower_equal = row_index >= col_index
    chunks = range(sub)
    part = [pl.ds(c * chunk, chunk) for c in chunks]

    for other in others():
        copy_small(other, other).wait_recv()
    pick = lax.broadcasted_iota(jnp.int32, (8, chunk), 0) == me
    ids, same, logit, rate, cont, in_last, last_cont = [], [], [], [], [], [], []
    before = None
    for c in chunks:
        block = sum(small[cores * c + p, 0:8, :] for p in range(cores))
        logit.append(column(jnp.sum(jnp.where(pick, block, 0.0), axis=0, keepdims=True)))
        rate.append(2.0 / (1.0 + jnp.exp(-logit[c])))
        id_row = small[cores * c, 8:9, :]
        id_col = column(id_row)
        ids.append(id_row)
        same.append(id_col == id_row)
        first = id_row[:, 0:1] if before is None else before
        cont.append(jnp.where(id_col == first, 1.0, 0.0).astype(f32))
        before = id_row[:, chunk - 1:chunk]
        in_last.append(jnp.where(id_col == before, 1.0, 0.0).astype(f32))
        last_cont.append(jnp.where(before == first, 1.0, 0.0).astype(f32))

    arrived(0)
    keys, key_scale, key, inverse = [], [], [], []
    system = []
    for c in chunks:
        unit_keys, scale = unit(kb[part[c], :].astype(f32))
        keys.append(unit_keys)
        key_scale.append(scale)
        key.append(split(unit_keys))
        gram = product(key[c], key[c], NT)
        system.append(rate[c] * jnp.where(same[c] & lower, gram, 0.0))
    size = 1
    while size < chunk:
        rb, cb = row_index // size, col_index // size
        off = (rb // 2 == cb // 2) & (rb > cb)
        if size == 1:
            inverse = [eye - jnp.where(off, system[c], 0.0) for c in chunks]
        else:
            pieces = [split(inverse[c]) for c in chunks]
            steps = [product(split(jnp.where(off, system[c], 0.0)), pieces[c]) for c in chunks]
            inverse = [inverse[c] - product(pieces[c], split(steps[c])) for c in chunks]
        size = size * 2
    inv = [split(inverse[c]) for c in chunks]

    arrived(1)
    joint, key_last, trans, offset = [], [], [], []
    for c in chunks:
        right = jnp.concatenate([rate[c] * cont[c] * keys[c], rate[c] * vb[part[c], :].astype(f32)], axis=1)
        joint.append(product(inv[c], split(right)))
    joint_s = [split(joint[c]) for c in chunks]
    for c in chunks:
        last = in_last[c].astype(bf16)
        key_last.append((key[c][0] * last, key[c][1] * last))
        both = product(key_last[c], joint_s[c], TN)
        trans.append(split(last_cont[c] * eye - both[:, :DK]))
        offset.append(both[:, DK:])

    if groups > 1:
        state = offset[0]
        for c in chunks[1:]:
            state = product(trans[c], split(state)) + offset[c]
        ahead_src[0:DK, :] = state
        ahead_src[DK:DK + 8, :] = jnp.broadcast_to(ids[-1][:, chunk - 1:chunk], (8, DK))

        def copy_ahead():
            return pltpu.make_async_remote_copy(
                src_ref=ahead_src, dst_ref=ahead, send_sem=send_state.at[0], recv_sem=recv_state.at[0],
                device_id={"ctx": ctx + sub}, device_id_type=MESH)

        def copy_back():
            return pltpu.make_async_remote_copy(
                src_ref=back_src, dst_ref=back, send_sem=send_state.at[1], recv_sem=recv_state.at[1],
                device_id={"ctx": ctx - sub}, device_id_type=MESH)

        @pl.when(group < groups - 1)
        def _():
            copy_ahead().start()

    arrived(2)
    queries, query_scale, query, scores = [], [], [], []
    for c in chunks:
        unit_queries, scale = unit(qb[part[c], :].astype(f32))
        queries.append(unit_queries)
        query_scale.append(scale)
        query.append(split(unit_queries))
        scores.append(split(jnp.where(same[c] & lower_equal, product(query[c], key[c], NT), 0.0)))
    reach, within = [], []
    for c in chunks:
        both = product(scores[c], joint_s[c])
        reach.append(split(cont[c] * queries[c] - both[:, :DK]))
        within.append(both[:, DK:])

    arrived(3)
    upstream = [(db[part[c], :], None) for c in chunks]
    response = [product(reach[c], upstream[c], TN) for c in chunks]
    if groups > 1:
        adjoint = response[-1]
        for c in reversed(chunks[:-1]):
            adjoint = product(trans[c], split(adjoint), TN) + response[c]
        back_src[0:DK, :] = adjoint
        back_src[DK:DK + 8, :] = jnp.broadcast_to(ids[0][:, 0:1], (8, DK))

        @pl.when(group > 0)
        def _():
            copy_back().start()

    direct = [product(scores[c], upstream[c], TN) for c in chunks]

    if groups > 1:
        @pl.when(group > 0)
        def _():
            copy_ahead().wait_recv()

        @pl.when(group == 0)
        def _():
            ahead[...] = jnp.zeros_like(ahead)

        @pl.when(group < groups - 1)
        def _():
            copy_back().wait_recv()

        @pl.when(group == groups - 1)
        def _():
            back[...] = jnp.zeros_like(back)

        first_state = jnp.where(ahead[DK:DK + 1, :] == ids[0][:, 0:1], ahead[0:DK, :], 0.0)
        last_adjoint = jnp.where(back[DK:DK + 1, :] == ids[-1][:, chunk - 1:chunk], back[0:DK, :], 0.0)
    else:
        first_state = jnp.zeros((DK, DK), f32)
        last_adjoint = jnp.zeros((DK, DK), f32)

    states = [split(first_state)]
    for c in chunks[:-1]:
        states.append(split(product(trans[c], states[c]) + offset[c]))
    adjoints = [None] * sub
    adjoints[-1] = split(last_adjoint)
    for c in reversed(chunks[:-1]):
        adjoints[c] = split(product(trans[c + 1], adjoints[c + 1], TN) + response[c + 1])

    def send_result(i, source_buffer, target):
        for other in others():
            copy_out(i, source_buffer, target, other, me).start()

    def copy_out(i, source_buffer, target, other, source):
        return pltpu.make_async_remote_copy(
            src_ref=source_buffer.at[rows(other), :], dst_ref=target.at[:, columns(source)],
            send_sem=send_out.at[i, other], recv_sem=recv_out.at[i, source],
            device_id=device(other), device_id_type=MESH)

    updates = []
    for c in chunks:
        weights = (joint_s[c][0][:, :DK], joint_s[c][1][:, :DK])
        both = product(stack(reach[c], weights), states[c])
        yb[part[c], :] = (within[c] + both[:chunk]).astype(bf16)
        updates.append(joint[c][:, DK:] - both[chunk:])
    send_result(0, yb, out_ref)
    update = [split(updates[c]) for c in chunks]

    targets = [product(inv[c], split(direct[c] + product(key_last[c], adjoints[c])), TN) for c in chunks]
    value_grads = [rate[c] * targets[c] for c in chunks]
    for c in chunks:
        gvb[part[c], :] = value_grads[c].astype(bf16)
    send_result(1, gvb, gv_ref)

    for c in chunks:
        lead = stack(split(value_grads[c]), upstream[c])
        both = product(lead, stack(update[c], states[c]), NT)
        gram_grad = jnp.where(same[c] & lower, both[:chunk, :chunk], 0.0)
        score_grad = split(jnp.where(same[c] & lower_equal, both[chunk:, :chunk], 0.0))
        around = split(-(gram_grad + jnp.transpose(gram_grad)))
        near = product(stack(score_grad, around), key[c])
        query_grad = near[:chunk] + cont[c] * both[chunk:, chunk:]
        key_grad = (
            near[chunk:] - cont[c] * both[:chunk, chunk:] + product(score_grad, query[c], TN)
            + in_last[c] * product(update[c], adjoints[c], NT)
        )
        query_grad = query_scale[c] * (
            query_grad - queries[c] * jnp.sum(queries[c] * query_grad, axis=1, keepdims=True))
        key_grad = key_scale[c] * (
            key_grad - keys[c] * jnp.sum(keys[c] * key_grad, axis=1, keepdims=True))
        gqb[part[c], :] = query_grad.astype(bf16)
        gkb[part[c], :] = key_grad.astype(bf16)
        logit_grad = jnp.sum(targets[c] * updates[c], axis=1, keepdims=True) / (1.0 + jnp.exp(logit[c]))
        rate_src[c] = jnp.transpose(logit_grad)[0:8, :]
    send_result(2, gqb, gq_ref)
    send_result(3, gkb, gk_ref)

    def copy_rate(other, source):
        return pltpu.make_async_remote_copy(
            src_ref=rate_src.at[other // cores], dst_ref=rate_in.at[source], send_sem=send_out.at[4, other],
            recv_sem=recv_out.at[4, source], device_id=device(other), device_id_type=MESH)

    for other in others():
        copy_rate(other, me).start()

    results = [(yb, out_ref), (gvb, gv_ref), (gqb, gq_ref), (gkb, gk_ref)]
    for buffer, target in results:
        target[:, columns(me)] = buffer[rows(me), :]
    rate_in[me] = rate_src[me // cores]

    for other in others():
        copy_rate(other, other).wait_recv()
    head_row = lax.broadcasted_iota(jnp.int32, (8, chunk), 0)
    gathered = sum(jnp.where(head_row == h, rate_in[h], 0.0) for h in range(count))
    spread = jnp.transpose(jnp.concatenate([gathered, jnp.zeros((chunk - 8, chunk), f32)], axis=0))
    mine = sum(jnp.where(core == p, spread[p * tokens:(p + 1) * tokens, :], 0.0) for p in range(cores))
    gb_ref[...] = mine[:, :count].astype(bf16)

    for i, (buffer, target) in enumerate(results):
        for other in others():
            copy_out(i, buffer, target, other, other).wait_recv()
    for other in others():
        copy_small(other, me).wait_send()
        copy_rate(other, me).wait_send()
        for i in range(4):
            copy_in(i, other, me).wait_send()
            copy_out(i, results[i][0], results[i][1], other, me).wait_send()
    if groups > 1:
        @pl.when(group < groups - 1)
        def _():
            copy_ahead().wait_send()

        @pl.when(group > 0)
        def _():
            copy_back().wait_send()


def on_device(query, key, value, beta_logit, turn_ids, d_out):
    cores = lax.axis_size("head")
    sub = HEAD_COUNT // cores
    groups = lax.axis_size("ctx") // sub
    tokens = query.shape[0]
    chunk = tokens * cores
    total = chunk * sub
    wide = jax.ShapeDtypeStruct(query.shape, bf16)
    vmem = pl.BlockSpec(memory_space=pltpu.VMEM)
    anywhere = pl.BlockSpec(memory_space=pl.ANY)
    dma = pltpu.SemaphoreType.DMA
    buffer = pltpu.VMEM((total, DK), bf16)
    state = pltpu.VMEM((DK + 8, DK), f32)
    return pl.pallas_call(
        functools.partial(kernel, groups, sub),
        out_shape=(wide, wide, wide, wide, jax.ShapeDtypeStruct(beta_logit.shape, bf16)),
        in_specs=[vmem, vmem] + [anywhere] * 4,
        out_specs=(vmem,) * 5,
        scratch_shapes=[
            pltpu.VMEM((16, chunk), f32),
            pltpu.VMEM((HEAD_COUNT, 16, chunk), f32),
            buffer, buffer, buffer, buffer,
            buffer, buffer, buffer, buffer,
            pltpu.VMEM((sub, 8, chunk), f32),
            pltpu.VMEM((HEAD_COUNT, 8, chunk), f32),
            state, state, state, state,
            dma((5, HEAD_COUNT)), dma((5, HEAD_COUNT)), dma((5, HEAD_COUNT)), dma((5, HEAD_COUNT)),
            dma((2,)), dma((2,)), dma((4,)),
        ],
        compiler_params=pltpu.CompilerParams(
            collective_id=0, has_side_effects=True, vmem_limit_bytes=48 * 1024 * 1024),
        cost_estimate=pl.CostEstimate(flops=1_500_000_000, bytes_accessed=2_000_000, transcendentals=100_000),
    )(turn_ids.reshape(1, chunk), beta_logit, query, key, value, d_out)


def solution(mesh):
    tokens = P(("grp", "ctx", "head"), None)
    return jax.shard_map(
        on_device,
        mesh=mesh,
        in_specs=(tokens, tokens, tokens, tokens, P(("grp", "ctx")), tokens),
        out_specs=(tokens,) * 5,
        check_vma=False,
    )
```

time: 467 us -> 39.3 us (0.08)
  waiting for transfers between devices: 184 us -> 0 us
  other arithmetic: 131 us -> 0 us
  matrix products: 57.8 us -> 0 us
  Pallas kernels: 0 us -> 30.7 us
  local copies, waits for them, and re-layouts: 34.3 us -> 7.67 us
  starting transfers between devices: 26.2 us -> 0 us
  blocking collectives: 15.4 us -> 0 us
  between operations: 15.7 us -> 0.66 us
    all_gather x4 -> x0, waiting for transfers between devices: 180 us -> none  [carried_in(): everything = jax.tree.map(lambda part: lax.all_gather(part, axis), shard)]
    another operation x14 -> x0, other arithmetic: 118 us -> none  [block_state(): lax.linalg.triangular_solve(system, targets, left_side=True, lower=True)]
    dot_general x70 -> x0, matrix products: 52.6 us -> none  [the longest x16 22.9 us: compose(): jnp.einsum('hij,hjk->hik', later[0], earlier[1], precision=highest)]
    pallas_call x0 -> x1, Pallas kernels: none -> 30.7 us  [on_device(): pl.pallas_call(functools.partial(kernel, groups, sub), out_shape=(wide, w...]
    all_to_all x6 -> x0, starting transfers between devices: 19.9 us -> none  [the longest x1 3.38 us: on_device(): lax.all_to_all(query, 'head', split_axis=1, concat_axis=0, tiled=True)]
    all_to_all x4 -> x0, blocking collectives: 15.4 us -> none  [the longest x1 3.84 us: on_device(): lax.all_to_all(grad_parts[1], 'head', split_axis=0, concat_axis=1, tiled=...]
    slice x14 -> x0, local copies, waits for them, and re-layouts: 8.87 us -> none  [the longest x6 3.5 us: block_state(): continues[length - 1] * state]
    select_n x18 -> x0, other arithmetic: 8.47 us -> none  [the longest x6 5.22 us: block_masks(): jnp.where(turn_block == turn_block[length - 1], 1.0, 0.0)]
  transfers between devices with their start and end apart: 11 -> 0, of which waited for: 8 -> 0; matrix products, arithmetic and copies ran while one was open for 6% -> 0% of each run, Pallas kernels for 0% -> 0%
where the time goes in v1:
time: 39.3 us; the launch traced here: 39 us
  Pallas kernels  30.7 us (78%)
  local copies, waits for them, and re-layouts  7.67 us (20%)
  between operations  0.66 us (2%)
    pallas_call x1, Pallas kernels, on_device(): pl.pallas_call(functools.partial(kernel, groups, sub), out_shape=(wide, w...  30.7 us
    unnamed x15, local copies, waits for them, and re-layouts  7.01 us

profile of v1, /device:TPU:0, one launch (start us, length us, event | category | flops | bytes accessed | tf_op | source)
XLA Modules:
  0.0 39.0 jit_solution(4275219307033250102)
XLA Ops:
  0.6 0.0 copy-start.4
  0.6 0.8 %copy.11.logit_ref = bf16[64,8]{1,0:T(8,128)(2,1)S(1)} copy(bf16[64,8]{0,1:T(8,128)(2,1)} %param.9) | data formatting | bytes 2048 | tf_op args[3]
  1.4 0.0 copy-done.4
  1.4 0.0 copy-start
  1.4 0.9 %copy-done = bf16[64,1024]{1,0:T(8,128)(2,1)S(1)} copy-done((bf16[64,1024]{1,0:T(8,128)(2,1)S(1)}, bf16[64,1024]{1,0:T(8,128)(2,1)}, u32[]{:S(2)}) %copy-start) | copy-done | bytes 131096
  2.3 0.0 copy-start.1
  2.3 0.9 %copy-done.1 = bf16[64,1024]{1,0:T(8,128)(2,1)S(1)} copy-done((bf16[64,1024]{1,0:T(8,128)(2,1)S(1)}, bf16[64,1024]{1,0:T(8,128)(2,1)}, u32[]{:S(2)}) %copy-start.1) | copy-done | bytes 131096
  3.2 0.0 copy-start.2
  3.2 0.9 %copy-done.2 = bf16[64,1024]{1,0:T(8,128)(2,1)S(1)} copy-done((bf16[64,1024]{1,0:T(8,128)(2,1)S(1)}, bf16[64,1024]{1,0:T(8,128)(2,1)}, u32[]{:S(2)}) %copy-start.2) | copy-done | bytes 131096
  4.1 0.0 copy-start.3
  4.1 0.9 %copy-done.3 = bf16[64,1024]{1,0:T(8,128)(2,1)S(1)} copy-done((bf16[64,1024]{1,0:T(8,128)(2,1)S(1)}, bf16[64,1024]{1,0:T(8,128)(2,1)}, u32[]{:S(2)}) %copy-start.3) | copy-done | bytes 131096
  5.0 30.7 %shard_map.101 = (bf16[64,1024]{1,0:T(8,128)(2,1)S(1)}, bf16[64,1024]{1,0:T(8,128)(2,1)S(1)}, bf16[64,1024]{1,0:T(8,128)(2,1)S(1)}, bf16[64,1024]{1,0:T(8,128)(2,1)S(1)}, bf16[64,8]{1,0:T(8,128)(2,1)S(1)}) custom-call(s32[1,128]{1,0:T(1,128)S(1)} %bitcast.1, bf16[64,8]{1,0:T(8,128)(2,1)S(1)} %copy.11.logit_ref, bf16[64,1024]{1,0:T(8,128)(2,1)S(1)} %copy-done, ...), custom_call_target="tpu_custom_call" | custom-call | flops 1500000000 | bytes 2000000 | tf_op jit(solution)/shard_map/pallas_call | solution.py:389
  35.8 0.7 %copy.12 = bf16[64,8]{0,1:T(8,128)(2,1)} copy(bf16[64,8]{1,0:T(8,128)(2,1)S(1)} %get-tuple-element.9) | data formatting | bytes 2048 | tf_op jit(solution)/shard_map/pallas_call | solution.py:389
  36.4 0.7 %copy.17 = bf16[64,1024]{1,0:T(8,128)(2,1)} copy(bf16[64,1024]{1,0:T(8,128)(2,1)S(1)} %get-tuple-element.15) | data formatting | bytes 262144
  37.1 0.7 %copy.18 = bf16[64,1024]{1,0:T(8,128)(2,1)} copy(bf16[64,1024]{1,0:T(8,128)(2,1)S(1)} %get-tuple-element.16) | data formatting | bytes 262144
  37.7 0.7 %copy.19 = bf16[64,1024]{1,0:T(8,128)(2,1)} copy(bf16[64,1024]{1,0:T(8,128)(2,1)S(1)} %get-tuple-element.17) | data formatting | bytes 262144
  38.4 0.7 %copy.20 = bf16[64,1024]{1,0:T(8,128)(2,1)} copy(bf16[64,1024]{1,0:T(8,128)(2,1)S(1)} %get-tuple-element.18) | data formatting | bytes 262144
Async XLA Ops:
  0.6 0.8 %copy-start.4 = (s32[128]{0:T(128)S(1)}, s32[128]{0:T(128)}, u32[]{:S(2)}) copy-start(s32[128]{0:T(128)} %param.10) | copy-start | bytes 1540
  1.4 0.9 %copy-start = (bf16[64,1024]{1,0:T(8,128)(2,1)S(1)}, bf16[64,1024]{1,0:T(8,128)(2,1)}, u32[]{:S(2)}) copy-start(bf16[64,1024]{1,0:T(8,128)(2,1)} %q_ref.1) | copy-start | bytes 393220
  2.3 0.9 %copy-start.1 = (bf16[64,1024]{1,0:T(8,128)(2,1)S(1)}, bf16[64,1024]{1,0:T(8,128)(2,1)}, u32[]{:S(2)}) copy-start(bf16[64,1024]{1,0:T(8,128)(2,1)} %k_ref.1) | copy-start | bytes 393220
  3.2 0.9 %copy-start.2 = (bf16[64,1024]{1,0:T(8,128)(2,1)S(1)}, bf16[64,1024]{1,0:T(8,128)(2,1)}, u32[]{:S(2)}) copy-start(bf16[64,1024]{1,0:T(8,128)(2,1)} %v_ref.1) | copy-start | bytes 393220
  4.1 0.9 %copy-start.3 = (bf16[64,1024]{1,0:T(8,128)(2,1)S(1)}, bf16[64,1024]{1,0:T(8,128)(2,1)}, u32[]{:S(2)}) copy-start(bf16[64,1024]{1,0:T(8,128)(2,1)} %d_ref.1) | copy-start | bytes 393220

commit v2 on v1

--- a/solution.py
+++ b/solution.py
@@ -59,9 +59,9 @@
 
 
 def kernel(
-    groups, sub, ids_ref, logit_ref, q_ref, k_ref, v_ref, d_ref,
+    groups, sub, ids_hbm, logit_hbm, q_ref, k_ref, v_ref, d_ref,
     out_ref, gq_ref, gk_ref, gv_ref, gb_ref,
-    small_src, small, kb, vb, qb, db, yb, gqb, gkb, gvb, rate_src, rate_in,
+    ids_ref, logit_ref, small_src, small, kb, vb, qb, db, yb, gqb, gkb, gvb, rate_src, rate_in,
     ahead_src, ahead, back_src, back,
     send_in, recv_in, send_out, recv_out, send_state, recv_state, local_sem,
 ):
@@ -105,12 +105,17 @@
         pltpu.make_async_copy(src.at[:, columns(me)], dst.at[rows(me), :], local_sem.at[i])
         for i, (src, dst) in enumerate(arrays)
     ]
-    for copy in own:
+    early = [
+        pltpu.make_async_copy(ids_hbm, ids_ref, local_sem.at[4]),
+        pltpu.make_async_copy(logit_hbm, logit_ref, local_sem.at[5]),
+    ]
+    for copy in early + own:
         copy.start()
-
-    logits = jnp.pad(logit_ref[...].astype(f32), ((0, 0), (0, DK - count)))
-    placed = jnp.concatenate([jnp.where(core == c, logits, 0.0) for c in range(cores)], axis=0)
-    small_src[0:8, :] = jnp.transpose(placed)[0:8, :]
+    for copy in early:
+        copy.wait()
+
+    logits = logit_ref[...].astype(f32)
+    small_src[0:8, :] = jnp.concatenate([jnp.where(core == c, logits, 0.0) for c in range(cores)], axis=1)
     small_src[8:16, :] = jnp.broadcast_to(ids_ref[...].astype(f32), (8, chunk))
     small[me] = small_src[...]
 
@@ -350,9 +355,8 @@
         copy_rate(other, other).wait_recv()
     head_row = lax.broadcasted_iota(jnp.int32, (8, chunk), 0)
     gathered = sum(jnp.where(head_row == h, rate_in[h], 0.0) for h in range(count))
-    spread = jnp.transpose(jnp.concatenate([gathered, jnp.zeros((chunk - 8, chunk), f32)], axis=0))
-    mine = sum(jnp.where(core == p, spread[p * tokens:(p + 1) * tokens, :], 0.0) for p in range(cores))
-    gb_ref[...] = mine[:, :count].astype(bf16)
+    mine = sum(jnp.where(core == p, gathered[:, p * tokens:(p + 1) * tokens], 0.0) for p in range(cores))
+    gb_ref[...] = mine.astype(bf16)
 
     for i, (buffer, target) in enumerate(results):
         for other in others():
@@ -371,6 +375,17 @@
         @pl.when(group > 0)
         def _():
             copy_back().wait_send()
+
+
+def place(*refs):
+    count = len(refs) // 2
+    copies = [
+        pltpu.make_async_copy(refs[i], refs[count + i], refs[-1].at[i]) for i in range(count)
+    ]
+    for copy in copies:
+        copy.start()
+    for copy in copies:
+        copy.wait()
 
 
 def on_device(query, key, value, beta_logit, turn_ids, d_out):
@@ -386,12 +401,16 @@
     dma = pltpu.SemaphoreType.DMA
     buffer = pltpu.VMEM((total, DK), bf16)
     state = pltpu.VMEM((DK + 8, DK), f32)
-    return pl.pallas_call(
+    hbm = pl.BlockSpec(memory_space=pltpu.HBM)
+    narrow = jax.ShapeDtypeStruct(beta_logit.shape[::-1], bf16)
+    results = pl.pallas_call(
         functools.partial(kernel, groups, sub),
-        out_shape=(wide, wide, wide, wide, jax.ShapeDtypeStruct(beta_logit.shape, bf16)),
-        in_specs=[vmem, vmem] + [anywhere] * 4,
+        out_shape=(wide, wide, wide, wide, narrow),
+        in_specs=[hbm] * 6,
         out_specs=(vmem,) * 5,
         scratch_shapes=[
+            pltpu.VMEM((1, chunk), jnp.int32),
+            pltpu.VMEM(narrow.shape, bf16),
             pltpu.VMEM((16, chunk), f32),
             pltpu.VMEM((HEAD_COUNT, 16, chunk), f32),
             buffer, buffer, buffer, buffer,
@@ -400,12 +419,21 @@
             pltpu.VMEM((HEAD_COUNT, 8, chunk), f32),
             state, state, state, state,
             dma((5, HEAD_COUNT)), dma((5, HEAD_COUNT)), dma((5, HEAD_COUNT)), dma((5, HEAD_COUNT)),
-            dma((2,)), dma((2,)), dma((4,)),
+            dma((2,)), dma((2,)), dma((6,)),
         ],
         compiler_params=pltpu.CompilerParams(
             collective_id=0, has_side_effects=True, vmem_limit_bytes=48 * 1024 * 1024),
         cost_estimate=pl.CostEstimate(flops=1_500_000_000, bytes_accessed=2_000_000, transcendentals=100_000),
-    )(turn_ids.reshape(1, chunk), beta_logit, query, key, value, d_out)
+    )(*(pltpu.with_memory_space_constraint(x, pltpu.HBM) for x in (turn_ids.reshape(1, chunk), beta_logit.T, query, key, value, d_out)))
+    results = pl.pallas_call(
+        place,
+        out_shape=(wide, wide, wide, wide, narrow),
+        in_specs=[anywhere] * 5,
+        out_specs=(hbm,) * 5,
+        scratch_shapes=[dma((5,))],
+        cost_estimate=pl.CostEstimate(flops=0, bytes_accessed=1_000_000, transcendentals=0),
+    )(*(pltpu.with_memory_space_constraint(x, pltpu.VMEM) for x in results))
+    return (*results[:4], results[4].T)
 
 
 def solution(mesh):

time: 39.3 us -> 32.7 us (0.83)
  local copies, waits for them, and re-layouts: 7.67 us -> 0 us
  Pallas kernels: 30.7 us -> 31.8 us
    unnamed x15 -> x0, local copies, waits for them, and re-layouts: 7.01 us -> none
    pallas_call x0 -> x1, Pallas kernels: none -> 0.83 us  [on_device(): pl.pallas_call(place, out_shape=(wide, wide, wide, wide, narrow), in_spec...]
    pallas_call x1 -> x0, local copies, waits for them, and re-layouts: 0.65 us -> none  [on_device(): pl.pallas_call(functools.partial(kernel, groups, sub), out_shape=(wide, w...]
where the time goes in v2:
time: 32.7 us; the launch traced here: 32.5 us
  Pallas kernels  31.8 us (97%)
  between operations  0.64 us (2%)
    pallas_call x1, Pallas kernels, on_device(): pl.pallas_call(functools.partial(kernel, groups, sub), out_shape=(wide, w...  31 us
    pallas_call x1, Pallas kernels, on_device(): pl.pallas_call(place, out_shape=(wide, wide, wide, wide, narrow), in_spec...  0.83 us

profile of v2, /device:TPU:0, one launch (start us, length us, event | category | flops | bytes accessed | tf_op | source)
XLA Modules:
  0.0 32.5 jit_solution(2907764052849755908)
XLA Ops:
  0.6 31.0 %shard_map.101 = (bf16[64,1024]{1,0:T(8,128)(2,1)S(1)}, bf16[64,1024]{1,0:T(8,128)(2,1)S(1)}, bf16[64,1024]{1,0:T(8,128)(2,1)S(1)}, bf16[64,1024]{1,0:T(8,128)(2,1)S(1)}, bf16[8,64]{1,0:T(8,128)(2,1)S(1)}) custom-call(s32[1,128]{1,0:T(1,128)} %bitcast.5, bf16[8,64]{1,0:T(8,128)(2,1)} %bitcast.3, bf16[64,1024]{1,0:T(8,128)(2,1)} %q_ref.1, ...), custom_call_target="tpu_custom_call" | custom-call | flops 1500000000 | bytes 2000000 | tf_op jit(solution)/shard_map/pallas_call | solution.py:406
  31.7 0.8 %shard_map.102 = (bf16[64,1024]{1,0:T(8,128)(2,1)}, bf16[64,1024]{1,0:T(8,128)(2,1)}, bf16[64,1024]{1,0:T(8,128)(2,1)}, bf16[64,1024]{1,0:T(8,128)(2,1)}, bf16[8,64]{1,0:T(8,128)(2,1)}) custom-call(bf16[64,1024]{1,0:T(8,128)(2,1)S(1)} %get-tuple-element.15.refs_0_, bf16[64,1024]{1,0:T(8,128)(2,1)S(1)} %get-tuple-element.16.refs_1_, ...), custom_call_target="tpu_custom_call" | custom-call | bytes 1000000 | tf_op jit(solution)/shard_map/pallas_call | solution.py:428

commit v3 on v2

v3 whole, which is shorter than its diff:
```python
import functools

import jax
import jax.numpy as jnp
from jax import lax
from jax.experimental import pallas as pl
from jax.experimental.pallas import tpu as pltpu
from jax.sharding import PartitionSpec as P

HEAD_COUNT = 8
DK = 128
epsilon = 1e-06
MESH = pl.DeviceIdType.MESH
f32 = jnp.float32
bf16 = jnp.bfloat16

NN = (((1,), (0,)), ((), ()))
NT = (((1,), (1,)), ((), ()))
TN = (((0,), (0,)), ((), ()))


def split(x):
    if x.dtype == bf16:
        return (x, None)
    high = x.astype(bf16)
    return (high, (x - high.astype(f32)).astype(bf16))


def product(a, b, dims=NN):
    left, right = [a[0]], [b[0]]
    if a[1] is not None:
        left.append(a[1])
        right.append(b[0])
    if b[1] is not None:
        left.append(a[0])
        right.append(b[1])
    (ca,), (cb,) = dims[0]
    left = jnp.concatenate(left, axis=ca) if len(left) > 1 else left[0]
    right = jnp.concatenate(right, axis=cb) if len(right) > 1 else right[0]
    return lax.dot_general(left, right, dims, preferred_element_type=f32)


def stack(a, b, axis=0):
    low = None
    if a[1] is not None or b[1] is not None:
        zero_a = jnp.zeros_like(a[0]) if a[1] is None else a[1]
        zero_b = jnp.zeros_like(b[0]) if b[1] is None else b[1]
        low = jnp.concatenate([zero_a, zero_b], axis=axis)
    return (jnp.concatenate([a[0], b[0]], axis=axis), low)


def unit(x):
    scale = lax.rsqrt(jnp.sum(x * x, axis=1, keepdims=True) + epsilon)
    return x * scale, scale


def column(row):
    return jnp.transpose(jnp.broadcast_to(row, (row.shape[1], row.shape[1])))


def kernel(
    groups, sub, ids_hbm, logit_hbm, q_ref, k_ref, v_ref, d_ref,
    first_out, second_out, gb_ref,
    ids_ref, logit_ref, first_src, second_src, first_in, second_in, first_back, second_back,
    ahead_src, ahead, back_src, back,
    send_in, recv_in, send_out, recv_out, send_state, recv_state, local_sem,
):
    count = HEAD_COUNT
    cores = count // sub
    tokens = q_ref.shape[0]
    chunk = tokens * cores
    ctx, core = lax.axis_index("ctx"), lax.axis_index("head")
    group = ctx // sub
    me = (ctx % sub) * cores + core

    def device(member):
        return {"ctx": group * sub + member // cores, "head": member % cores}

    def others():
        return [lax.rem(me + d, count) for d in range(1, count)]

    def columns(member):
        return pl.ds(pl.multiple_of(member * DK, DK), DK)

    def rows(member):
        return pl.ds(pl.multiple_of(member * tokens, tokens), tokens)

    barrier = pltpu.get_barrier_semaphore()
    for other in others():
        pl.semaphore_signal(barrier, inc=1, device_id=device(other), device_id_type=MESH)
    waits = count - 1
    if groups > 1:
        @pl.when(group > 0)
        def _():
            pl.semaphore_signal(barrier, inc=1, device_id={"ctx": ctx - sub}, device_id_type=MESH)

        @pl.when(group < groups - 1)
        def _():
            pl.semaphore_signal(barrier, inc=1, device_id={"ctx": ctx + sub}, device_id_type=MESH)

        waits = waits + (group + groups - 1) // groups + (groups - 1 - group + groups - 1) // groups

    own = [
        pltpu.make_async_copy(src, dst.at[pl.ds(start, tokens), :], local_sem.at[i])
        for i, (src, dst, start) in enumerate([
            (k_ref, first_src, 0), (v_ref, second_src, 0),
            (q_ref, second_src, tokens), (d_ref, second_src, 2 * tokens)])
    ]
    early = [
        pltpu.make_async_copy(ids_hbm, ids_ref, local_sem.at[4]),
        pltpu.make_async_copy(logit_hbm, logit_ref, local_sem.at[5]),
    ]
    for copy in early + own:
        copy.start()
    for copy in early:
        copy.wait()

    logits = logit_ref[...].astype(f32)
    logits = jnp.concatenate([jnp.where(core == c, logits, 0.0) for c in range(cores)], axis=1)
    turns = jnp.broadcast_to(ids_ref[...].astype(f32), (8, chunk))
    extra = jnp.concatenate([logits, turns], axis=0).astype(bf16)
    for member in range(count):
        first_src[tokens:tokens + 16, member * DK:(member + 1) * DK] = extra

    def copy_in(i, other, source):
        src, dst = [(first_src, first_in), (second_src, second_in)][i]
        return pltpu.make_async_remote_copy(
            src_ref=src.at[:, columns(other)], dst_ref=dst.at[source], send_sem=send_in.at[i, other],
            recv_sem=recv_in.at[i, source], device_id=device(other), device_id_type=MESH)

    own[0].wait()
    pl.semaphore_wait(barrier, waits)
    for other in others():
        copy_in(0, other, me).start()
    for copy in own[1:]:
        copy.wait()
    for other in others():
        copy_in(1, other, me).start()
    first_in[me] = first_src[:, columns(me)]
    second_in[me] = second_src[:, columns(me)]

    def arrived(i):
        for other in others():
            copy_in(i, other, other).wait_recv()

    def block_of(buffer, start, c):
        return jnp.concatenate([buffer[cores * c + p, start:start + tokens, :] for p in range(cores)], axis=0)

    def put(buffer, start, c, value):
        for p in range(cores):
            buffer[cores * c + p, start:start + tokens, :] = value[p * tokens:(p + 1) * tokens].astype(bf16)

    row_index = lax.broadcasted_iota(jnp.int32, (chunk, chunk), 0)
    col_index = lax.broadcasted_iota(jnp.int32, (chunk, chunk), 1)
    eye = jnp.where(row_index == col_index, 1.0, 0.0).astype(f32)
    lower = row_index > col_index
    lower_equal = row_index >= col_index
    chunks = range(sub)

    arrived(0)
    pick = lax.broadcasted_iota(jnp.int32, (8, chunk), 0) == me
    ids, same, logit, rate, cont, in_last, last_cont = [], [], [], [], [], [], []
    before = None
    for c in chunks:
        extras = [first_in[cores * c + p, tokens:tokens + 16, :].astype(f32) for p in range(cores)]
        block = sum(extras[p][0:8, :] for p in range(cores))
        logit.append(column(jnp.sum(jnp.where(pick, block, 0.0), axis=0, keepdims=True)))
        rate.append(2.0 / (1.0 + jnp.exp(-logit[c])))
        id_row = extras[0][8:9, :]
        id_col = column(id_row)
        ids.append(id_row)
        same.append(id_col == id_row)
        first = id_row[:, 0:1] if before is None else before
        cont.append(jnp.where(id_col == first, 1.0, 0.0).astype(f32))
        before = id_row[:, chunk - 1:chunk]
        in_last.append(jnp.where(id_col == before, 1.0, 0.0).astype(f32))
        last_cont.append(jnp.where(before == first, 1.0, 0.0).astype(f32))

    keys, key_scale, key, inverse = [], [], [], []
    system = []
    for c in chunks:
        unit_keys, scale = unit(block_of(first_in, 0, c).astype(f32))
        keys.append(unit_keys)
        key_scale.append(scale)
        key.append(split(unit_keys))
        gram = product(key[c], key[c], NT)
        system.append(rate[c] * jnp.where(same[c] & lower, gram, 0.0))
    size = 1
    while size < chunk:
        rb, cb = row_index // size, col_index // size
        off = (rb // 2 == cb // 2) & (rb > cb)
        if size == 1:
            inverse = [eye - jnp.where(off, system[c], 0.0) for c in chunks]
        else:
            pieces = [split(inverse[c]) for c in chunks]
            steps = [product(split(jnp.where(off, system[c], 0.0)), pieces[c]) for c in chunks]
            inverse = [inverse[c] - product(pieces[c], split(steps[c])) for c in chunks]
        size = size * 2
    inv = [split(inverse[c]) for c in chunks]

    arrived(1)
    joint, key_last, trans, offset = [], [], [], []
    for c in chunks:
        right = jnp.concatenate([rate[c] * cont[c] * keys[c], rate[c] * block_of(second_in, 0, c).astype(f32)], axis=1)
        joint.append(product(inv[c], split(right)))
    joint_s = [split(joint[c]) for c in chunks]
    for c in chunks:
        last = in_last[c].astype(bf16)
        key_last.append((key[c][0] * last, key[c][1] * last))
        both = product(key_last[c], joint_s[c], TN)
        trans.append(split(last_cont[c] * eye - both[:, :DK]))
        offset.append(both[:, DK:])

    if groups > 1:
        state = offset[0]
        for c in chunks[1:]:
            state = product(trans[c], split(state)) + offset[c]
        ahead_src[0:DK, :] = state
        ahead_src[DK:DK + 8, :] = jnp.broadcast_to(ids[-1][:, chunk - 1:chunk], (8, DK))

        def copy_ahead():
            return pltpu.make_async_remote_copy(
                src_ref=ahead_src, dst_ref=ahead, send_sem=send_state.at[0], recv_sem=recv_state.at[0],
                device_id={"ctx": ctx + sub}, device_id_type=MESH)

        def copy_back():
            return pltpu.make_async_remote_copy(
                src_ref=back_src, dst_ref=back, send_sem=send_state.at[1], recv_sem=recv_state.at[1],
                device_id={"ctx": ctx - sub}, device_id_type=MESH)

        @pl.when(group < groups - 1)
        def _():
            copy_ahead().start()

    queries, query_scale, query, scores = [], [], [], []
    for c in chunks:
        unit_queries, scale = unit(block_of(second_in, tokens, c).astype(f32))
        queries.append(unit_queries)
        query_scale.append(scale)
        query.append(split(unit_queries))
        scores.append(split(jnp.where(same[c] & lower_equal, product(query[c], key[c], NT), 0.0)))
    reach, within = [], []
    for c in chunks:
        both = product(scores[c], joint_s[c])
        reach.append(split(cont[c] * queries[c] - both[:, :DK]))
        within.append(both[:, DK:])

    upstream = [(block_of(second_in, 2 * tokens, c), None) for c in chunks]
    response = [product(reach[c], upstream[c], TN) for c in chunks]
    if groups > 1:
        adjoint = response[-1]
        for c in reversed(chunks[:-1]):
            adjoint = product(trans[c], split(adjoint), TN) + response[c]
        back_src[0:DK, :] = adjoint
        back_src[DK:DK + 8, :] = jnp.broadcast_to(ids[0][:, 0:1], (8, DK))

        @pl.when(group > 0)
        def _():
            copy_back().start()

    direct = [product(scores[c], upstream[c], TN) for c in chunks]

    if groups > 1:
        @pl.when(group > 0)
        def _():
            copy_ahead().wait_recv()

        @pl.when(group == 0)
        def _():
            ahead[...] = jnp.zeros_like(ahead)

        first_state = jnp.where(ahead[DK:DK + 1, :] == ids[0][:, 0:1], ahead[0:DK, :], 0.0)
    else:
        first_state = jnp.zeros((DK, DK), f32)

    states = [split(first_state)]
    for c in chunks[:-1]:
        states.append(split(product(trans[c], states[c]) + offset[c]))

    results = [(first_back, first_out), (second_back, second_out)]

    def copy_out(i, other, source):
        return pltpu.make_async_remote_copy(
            src_ref=results[i][0].at[other], dst_ref=results[i][1].at[:, columns(source)],
            send_sem=send_out.at[i, other], recv_sem=recv_out.at[i, source],
            device_id=device(other), device_id_type=MESH)

    def send_result(i):
        for other in others():
            copy_out(i, other, me).start()

    updates = []
    for c in chunks:
        weights = (joint_s[c][0][:, :DK], joint_s[c][1][:, :DK])
        both = product(stack(reach[c], weights), states[c])
        put(first_back, 0, c, within[c] + both[:chunk])
        updates.append(joint[c][:, DK:] - both[chunk:])
    update = [split(updates[c]) for c in chunks]

    both_side, score_grad = [], []
    for c in chunks:
        both_side.append(stack(update[c], states[c]))
        both = product(upstream[c], both_side[c], NT)
        score_grad.append(split(jnp.where(same[c] & lower_equal, both[:, :chunk], 0.0)))
        query_grad = product(score_grad[c], key[c]) + cont[c] * both[:, chunk:]
        query_grad = query_scale[c] * (
            query_grad - queries[c] * jnp.sum(queries[c] * query_grad, axis=1, keepdims=True))
        put(first_back, tokens, c, query_grad)
    send_result(0)
    cross = [product(score_grad[c], query[c], TN) for c in chunks]

    if groups > 1:
        @pl.when(group < groups - 1)
        def _():
            copy_back().wait_recv()

        @pl.when(group == groups - 1)
        def _():
            back[...] = jnp.zeros_like(back)

        last_adjoint = jnp.where(back[DK:DK + 1, :] == ids[-1][:, chunk - 1:chunk], back[0:DK, :], 0.0)
    else:
        last_adjoint = jnp.zeros((DK, DK), f32)
    adjoints = [None] * sub
    adjoints[-1] = split(last_adjoint)
    for c in reversed(chunks[:-1]):
        adjoints[c] = split(product(trans[c + 1], adjoints[c + 1], TN) + response[c + 1])

    targets = [product(inv[c], split(direct[c] + product(key_last[c], adjoints[c])), TN) for c in chunks]
    value_grads = [rate[c] * targets[c] for c in chunks]
    for c in chunks:
        put(second_back, 0, c, value_grads[c])

    for c in chunks:
        both = product(split(value_grads[c]), both_side[c], NT)
        gram_grad = jnp.where(same[c] & lower, both[:, :chunk], 0.0)
        around = split(-(gram_grad + jnp.transpose(gram_grad)))
        key_grad = (
            product(around, key[c]) - cont[c] * both[:, chunk:] + cross[c]
            + in_last[c] * product(update[c], adjoints[c], NT)
        )
        key_grad = key_scale[c] * (
            key_grad - keys[c] * jnp.sum(keys[c] * key_grad, axis=1, keepdims=True))
        put(second_back, tokens, c, key_grad)
        logit_grad = jnp.sum(targets[c] * updates[c], axis=1, keepdims=True) / (1.0 + jnp.exp(logit[c]))
        logit_rows = jnp.transpose(logit_grad)[0:16, :].astype(bf16)
        for p in range(cores):
            second_back[cores * c + p, 2 * tokens:2 * tokens + 16, :] = logit_rows
    send_result(1)

    for i, (buffer, target) in enumerate(results):
        target[:, columns(me)] = buffer[me]
        for other in others():
            copy_out(i, other, other).wait_recv()
    head_row = lax.broadcasted_iota(jnp.int32, (8, chunk), 0)
    gathered = sum(
        jnp.where(head_row == h, second_out[2 * tokens:2 * tokens + 16, h * DK:(h + 1) * DK].astype(f32)[0:8], 0.0)
        for h in range(count))
    mine = sum(jnp.where(core == p, gathered[:, p * tokens:(p + 1) * tokens], 0.0) for p in range(cores))
    gb_ref[...] = mine.astype(bf16)

    for other in others():
        for i in range(2):
            copy_in(i, other, me).wait_send()
            copy_out(i, other, me).wait_send()
    if groups > 1:
        @pl.when(group < groups - 1)
        def _():
            copy_ahead().wait_send()

        @pl.when(group > 0)
        def _():
            copy_back().wait_send()


def place(first, second, narrow, out, gq, gk, gv, gb, sem):
    tokens = out.shape[0]
    head, tail = pl.ds(0, tokens), pl.ds(tokens, tokens)
    pairs = [
        (first.at[head, :], out), (first.at[tail, :], gq), (second.at[tail, :], gk),
        (second.at[head, :], gv), (narrow, gb)]
    copies = [pltpu.make_async_copy(src, dst, sem.at[i]) for i, (src, dst) in enumerate(pairs)]
    for copy in copies:
        copy.start()
    for copy in copies:
        copy.wait()


def on_device(query, key, value, beta_logit, turn_ids, d_out):
    cores = lax.axis_size("head")
    sub = HEAD_COUNT // cores
    groups = lax.axis_size("ctx") // sub
    tokens = query.shape[0]
    chunk = tokens * cores
    width = query.shape[1]
    wide = jax.ShapeDtypeStruct(query.shape, bf16)
    vmem = pl.BlockSpec(memory_space=pltpu.VMEM)
    anywhere = pl.BlockSpec(memory_space=pl.ANY)
    dma = pltpu.SemaphoreType.DMA
    rows = (tokens + 16, 3 * tokens, 2 * tokens, 2 * tokens + 16)
    state = pltpu.VMEM((DK + 8, DK), f32)
    hbm = pl.BlockSpec(memory_space=pltpu.HBM)
    narrow = jax.ShapeDtypeStruct(beta_logit.shape[::-1], bf16)
    results = pl.pallas_call(
        functools.partial(kernel, groups, sub),
        out_shape=(*(jax.ShapeDtypeStruct((n, width), bf16) for n in rows[2:]), narrow),
        in_specs=[hbm] * 6,
        out_specs=(vmem,) * 3,
        scratch_shapes=[
            pltpu.VMEM((1, chunk), jnp.int32),
            pltpu.VMEM(narrow.shape, bf16),
            *(pltpu.VMEM((n, width), bf16) for n in rows[:2]),
            *(pltpu.VMEM((HEAD_COUNT, n, DK), bf16) for n in rows),
            state, state, state, state,
            *(dma((2, HEAD_COUNT)) for _ in range(4)),
            dma((2,)), dma((2,)), dma((6,)),
        ],
        compiler_params=pltpu.CompilerParams(
            collective_id=0, has_side_effects=True, vmem_limit_bytes=48 * 1024 * 1024),
        cost_estimate=pl.CostEstimate(flops=1_500_000_000, bytes_accessed=2_000_000, transcendentals=100_000),
    )(*(pltpu.with_memory_space_constraint(x, pltpu.HBM) for x in (turn_ids.reshape(1, chunk), beta_logit.T, query, key, value, d_out)))
    results = pl.pallas_call(
        place,
        out_shape=(wide, wide, wide, wide, narrow),
        in_specs=[anywhere] * 3,
        out_specs=(hbm,) * 5,
        scratch_shapes=[dma((5,))],
        cost_estimate=pl.CostEstimate(flops=0, bytes_accessed=1_000_000, transcendentals=0),
    )(*(pltpu.with_memory_space_constraint(x, pltpu.VMEM) for x in results))
    return (*results[:4], results[4].T)


def solution(mesh):
    tokens = P(("grp", "ctx", "head"), None)
    return jax.shard_map(
        on_device,
        mesh=mesh,
        in_specs=(tokens, tokens, tokens, tokens, P(("grp", "ctx")), tokens),
        out_specs=(tokens,) * 5,
        check_vma=False,
    )
```

time: 32.7 us -> 29.9 us (0.914)
  Pallas kernels: 31.8 us -> 29.1 us
    pallas_call x1, Pallas kernels: 31 us -> 28.3 us  [on_device(): pl.pallas_call(functools.partial(kernel, groups, sub), out_shape=(*(jax.S...]
where the time goes in v3:
time: 29.9 us; the launch traced here: 29.7 us
  Pallas kernels  29.1 us (97%)
  between operations  0.64 us (2%)
    pallas_call x1, Pallas kernels, on_device(): pl.pallas_call(functools.partial(kernel, groups, sub), out_shape=(*(jax.S...  28.3 us
    pallas_call x1, Pallas kernels, on_device(): pl.pallas_call(place, out_shape=(wide, wide, wide, wide, narrow), in_spec...  0.83 us

profile of v3, /device:TPU:0, one launch (start us, length us, event | category | flops | bytes accessed | tf_op | source)
XLA Modules:
  0.0 29.7 jit_solution(3630194837095295486)
XLA Ops:
  0.6 28.3 %shard_map.101 = (bf16[128,1024]{1,0:T(8,128)(2,1)S(1)}, bf16[144,1024]{1,0:T(8,128)(2,1)S(1)}, bf16[8,64]{1,0:T(8,128)(2,1)S(1)}) custom-call(s32[1,128]{1,0:T(1,128)} %bitcast.5, bf16[8,64]{1,0:T(8,128)(2,1)} %bitcast.3, bf16[64,1024]{1,0:T(8,128)(2,1)} %q_ref.1, bf16[64,1024]{1,0:T(8,128)(2,1)} %k_ref.1, bf16[64,1024]{1,0:T(8,128)(2,1)} %v_ref.1, ...), custom_call_target="tpu_custom_call" | custom-call | flops 1500000000 | bytes 2000000 | tf_op jit(solution)/shard_map/pallas_call | solution.py:404
  28.9 0.8 %shard_map.102 = (bf16[64,1024]{1,0:T(8,128)(2,1)}, bf16[64,1024]{1,0:T(8,128)(2,1)}, bf16[64,1024]{1,0:T(8,128)(2,1)}, bf16[64,1024]{1,0:T(8,128)(2,1)}, bf16[8,64]{1,0:T(8,128)(2,1)}) custom-call(bf16[128,1024]{1,0:T(8,128)(2,1)S(1)} %get-tuple-element.13.first, bf16[144,1024]{1,0:T(8,128)(2,1)S(1)} %get-tuple-element.14.second, ...), custom_call_target="tpu_custom_call" | custom-call | bytes 1000000 | tf_op jit(solution)/shard_map/pallas_call | solution.py:422

commit v4 on v3

--- a/solution.py
+++ b/solution.py
@@ -103,8 +103,8 @@
     own = [
         pltpu.make_async_copy(src, dst.at[pl.ds(start, tokens), :], local_sem.at[i])
         for i, (src, dst, start) in enumerate([
-            (k_ref, first_src, 0), (v_ref, second_src, 0),
-            (q_ref, second_src, tokens), (d_ref, second_src, 2 * tokens)])
+            (k_ref, first_src, 0), (q_ref, second_src, 0),
+            (v_ref, second_src, tokens), (d_ref, second_src, 2 * tokens)])
     ]
     early = [
         pltpu.make_async_copy(ids_hbm, ids_ref, local_sem.at[4]),
@@ -123,9 +123,11 @@
         first_src[tokens:tokens + 16, member * DK:(member + 1) * DK] = extra
 
     def copy_in(i, other, source):
-        src, dst = [(first_src, first_in), (second_src, second_in)][i]
+        src, dst, start, size = [
+            (first_src, first_in, 0, tokens + 16), (second_src, second_in, 0, tokens),
+            (second_src, second_in, tokens, 2 * tokens)][i]
         return pltpu.make_async_remote_copy(
-            src_ref=src.at[:, columns(other)], dst_ref=dst.at[source], send_sem=send_in.at[i, other],
+            src_ref=src.at[pl.ds(start, size), columns(other)], dst_ref=dst.at[source, pl.ds(start, size), :], send_sem=send_in.at[i, other],
             recv_sem=recv_in.at[i, source], device_id=device(other), device_id_type=MESH)
 
     own[0].wait()
@@ -134,8 +136,9 @@
         copy_in(0, other, me).start()
     for copy in own[1:]:
         copy.wait()
-    for other in others():
-        copy_in(1, other, me).start()
+    for i in (1, 2):
+        for other in others():
+            copy_in(i, other, me).start()
     first_in[me] = first_src[:, columns(me)]
     second_in[me] = second_src[:, columns(me)]
 
@@ -198,26 +201,43 @@
         size = size * 2
     inv = [split(inverse[c]) for c in chunks]
 
-    arrived(1)
-    joint, key_last, trans, offset = [], [], [], []
-    for c in chunks:
-        right = jnp.concatenate([rate[c] * cont[c] * keys[c], rate[c] * block_of(second_in, 0, c).astype(f32)], axis=1)
-        joint.append(product(inv[c], split(right)))
-    joint_s = [split(joint[c]) for c in chunks]
-    for c in chunks:
+    weight, key_last, trans = [], [], []
+    for c in chunks:
+        weight.append(split(product(inv[c], split(rate[c] * cont[c] * keys[c]))))
         last = in_last[c].astype(bf16)
         key_last.append((key[c][0] * last, key[c][1] * last))
-        both = product(key_last[c], joint_s[c], TN)
-        trans.append(split(last_cont[c] * eye - both[:, :DK]))
-        offset.append(both[:, DK:])
+        trans.append(split(last_cont[c] * eye - product(key_last[c], weight[c], TN)))
+    from_start = [None, trans[0]]
+    for c in chunks[1:-1]:
+        from_start.append(split(product(trans[c], from_start[c])))
+    to_end = [None] * sub
+    to_end[-2] = trans[-1]
+    for c in reversed(chunks[:-2]):
+        to_end[c] = split(product(to_end[c + 1], trans[c + 1]))
+
+    arrived(1)
+    queries, query_scale, query, scores, reach = [], [], [], [], []
+    for c in chunks:
+        unit_queries, scale = unit(block_of(second_in, 0, c).astype(f32))
+        queries.append(unit_queries)
+        query_scale.append(scale)
+        query.append(split(unit_queries))
+        scores.append(split(jnp.where(same[c] & lower_equal, product(query[c], key[c], NT), 0.0)))
+    for c in chunks:
+        reach.append(split(cont[c] * queries[c] - product(scores[c], weight[c])))
+
+    arrived(2)
+    upstream = [(block_of(second_in, 2 * tokens, c), None) for c in chunks]
+    response = [product(reach[c], upstream[c], TN) for c in chunks]
+    fresh, offset = [], []
+    for c in chunks:
+        fresh.append(product(inv[c], split(rate[c] * block_of(second_in, tokens, c).astype(f32))))
+    fresh_s = [split(fresh[c]) for c in chunks]
+    offset = [product(key_last[c], fresh_s[c], TN) for c in chunks]
+    response_s = [split(response[c]) for c in chunks]
+    offset_s = [split(offset[c]) for c in chunks]
 
     if groups > 1:
-        state = offset[0]
-        for c in chunks[1:]:
-            state = product(trans[c], split(state)) + offset[c]
-        ahead_src[0:DK, :] = state
-        ahead_src[DK:DK + 8, :] = jnp.broadcast_to(ids[-1][:, chunk - 1:chunk], (8, DK))
-
         def copy_ahead():
             return pltpu.make_async_remote_copy(
                 src_ref=ahead_src, dst_ref=ahead, send_sem=send_state.at[0], recv_sem=recv_state.at[0],
@@ -228,36 +248,28 @@
                 src_ref=back_src, dst_ref=back, send_sem=send_state.at[1], recv_sem=recv_state.at[1],
                 device_id={"ctx": ctx - sub}, device_id_type=MESH)
 
+        ahead_src[0:DK, :] = offset[-1] + sum(product(to_end[c], offset_s[c]) for c in chunks[:-1])
+        ahead_src[DK:DK + 8, :] = jnp.broadcast_to(ids[-1][:, chunk - 1:chunk], (8, DK))
+
         @pl.when(group < groups - 1)
         def _():
             copy_ahead().start()
 
-    queries, query_scale, query, scores = [], [], [], []
-    for c in chunks:
-        unit_queries, scale = unit(block_of(second_in, tokens, c).astype(f32))
-        queries.append(unit_queries)
-        query_scale.append(scale)
-        query.append(split(unit_queries))
-        scores.append(split(jnp.where(same[c] & lower_equal, product(query[c], key[c], NT), 0.0)))
-    reach, within = [], []
-    for c in chunks:
-        both = product(scores[c], joint_s[c])
-        reach.append(split(cont[c] * queries[c] - both[:, :DK]))
-        within.append(both[:, DK:])
-
-    upstream = [(block_of(second_in, 2 * tokens, c), None) for c in chunks]
-    response = [product(reach[c], upstream[c], TN) for c in chunks]
-    if groups > 1:
-        adjoint = response[-1]
-        for c in reversed(chunks[:-1]):
-            adjoint = product(trans[c], split(adjoint), TN) + response[c]
-        back_src[0:DK, :] = adjoint
+        back_src[0:DK, :] = response[0] + sum(product(from_start[c], response_s[c], TN) for c in chunks[1:])
         back_src[DK:DK + 8, :] = jnp.broadcast_to(ids[0][:, 0:1], (8, DK))
 
         @pl.when(group > 0)
         def _():
             copy_back().start()
 
+    within = [product(scores[c], fresh_s[c]) for c in chunks]
+    own_state = [None, offset[0]]
+    for c in chunks[1:-1]:
+        own_state.append(product(trans[c], split(own_state[c])) + offset[c])
+    own_adjoint = [None] * sub
+    own_adjoint[-2] = response[-1]
+    for c in reversed(chunks[:-2]):
+        own_adjoint[c] = product(trans[c + 1], split(own_adjoint[c + 1]), TN) + response[c + 1]
     direct = [product(scores[c], upstream[c], TN) for c in chunks]
 
     if groups > 1:
@@ -274,14 +286,17 @@
         first_state = jnp.zeros((DK, DK), f32)
 
     states = [split(first_state)]
-    for c in chunks[:-1]:
-        states.append(split(product(trans[c], states[c]) + offset[c]))
+    for c in chunks[1:]:
+        states.append(split(product(from_start[c], states[0]) + own_state[c]))
 
     results = [(first_back, first_out), (second_back, second_out)]
 
     def copy_out(i, other, source):
+        src, dst, start, size = [
+            (first_back, first_out, 0, 2 * tokens), (second_back, second_out, 0, tokens),
+            (second_back, second_out, tokens, tokens + 16)][i]
         return pltpu.make_async_remote_copy(
-            src_ref=results[i][0].at[other], dst_ref=results[i][1].at[:, columns(source)],
+            src_ref=src.at[other, pl.ds(start, size), :], dst_ref=dst.at[pl.ds(start, size), columns(source)],
             send_sem=send_out.at[i, other], recv_sem=recv_out.at[i, source],
             device_id=device(other), device_id_type=MESH)
 
@@ -291,10 +306,9 @@
 
     updates = []
     for c in chunks:
-        weights = (joint_s[c][0][:, :DK], joint_s[c][1][:, :DK])
-        both = product(stack(reach[c], weights), states[c])
+        both = product(stack(reach[c], weight[c]), states[c])
         put(first_back, 0, c, within[c] + both[:chunk])
-        updates.append(joint[c][:, DK:] - both[chunk:])
+        updates.append(fresh[c] - both[chunk:])
     update = [split(updates[c]) for c in chunks]
 
     both_side, score_grad = [], []
@@ -323,13 +337,14 @@
         last_adjoint = jnp.zeros((DK, DK), f32)
     adjoints = [None] * sub
     adjoints[-1] = split(last_adjoint)
-    for c in reversed(chunks[:-1]):
-        adjoints[c] = split(product(trans[c + 1], adjoints[c + 1], TN) + response[c + 1])
+    for c in chunks[:-1]:
+        adjoints[c] = split(product(to_end[c], adjoints[-1], TN) + own_adjoint[c])
 
     targets = [product(inv[c], split(direct[c] + product(key_last[c], adjoints[c])), TN) for c in chunks]
     value_grads = [rate[c] * targets[c] for c in chunks]
     for c in chunks:
         put(second_back, 0, c, value_grads[c])
+    send_result(1)
 
     for c in chunks:
         both = product(split(value_grads[c]), both_side[c], NT)
@@ -346,10 +361,11 @@
         logit_rows = jnp.transpose(logit_grad)[0:16, :].astype(bf16)
         for p in range(cores):
             second_back[cores * c + p, 2 * tokens:2 * tokens + 16, :] = logit_rows
-    send_result(1)
-
-    for i, (buffer, target) in enumerate(results):
+    send_result(2)
+
+    for buffer, target in results:
         target[:, columns(me)] = buffer[me]
+    for i in range(3):
         for other in others():
             copy_out(i, other, other).wait_recv()
     head_row = lax.broadcasted_iota(jnp.int32, (8, chunk), 0)
@@ -360,7 +376,7 @@
     gb_ref[...] = mine.astype(bf16)
 
     for other in others():
-        for i in range(2):
+        for i in range(3):
             copy_in(i, other, me).wait_send()
             copy_out(i, other, me).wait_send()
     if groups > 1:
@@ -412,7 +428,7 @@
             *(pltpu.VMEM((n, width), bf16) for n in rows[:2]),
             *(pltpu.VMEM((HEAD_COUNT, n, DK), bf16) for n in rows),
             state, state, state, state,
-            *(dma((2, HEAD_COUNT)) for _ in range(4)),
+            *(dma((3, HEAD_COUNT)) for _ in range(4)),
             dma((2,)), dma((2,)), dma((6,)),
         ],
         compiler_params=pltpu.CompilerParams(

time: 29.9 us -> 29.4 us (0.983)
  Pallas kernels: 29.1 us -> 28.6 us
    pallas_call x1, Pallas kernels: 28.3 us -> 27.8 us  [on_device(): pl.pallas_call(functools.partial(kernel, groups, sub), out_shape=(*(jax.S...]
where the time goes in v4:
time: 29.4 us; the launch traced here: 29.2 us
  Pallas kernels  28.6 us (97%)
  between operations  0.64 us (2%)
    pallas_call x1, Pallas kernels, on_device(): pl.pallas_call(functools.partial(kernel, groups, sub), out_shape=(*(jax.S...  27.8 us
    pallas_call x1, Pallas kernels, on_device(): pl.pallas_call(place, out_shape=(wide, wide, wide, wide, narrow), in_spec...  0.83 us

profile of v4, /device:TPU:0, one launch (start us, length us, event | category | flops | bytes accessed | tf_op | source)
XLA Modules:
  0.0 29.2 jit_solution(3712524239141501266)
XLA Ops:
  0.6 27.8 %shard_map.101 = (bf16[128,1024]{1,0:T(8,128)(2,1)S(1)}, bf16[144,1024]{1,0:T(8,128)(2,1)S(1)}, bf16[8,64]{1,0:T(8,128)(2,1)S(1)}) custom-call(s32[1,128]{1,0:T(1,128)} %bitcast.5, bf16[8,64]{1,0:T(8,128)(2,1)} %bitcast.3, bf16[64,1024]{1,0:T(8,128)(2,1)} %q_ref.1, bf16[64,1024]{1,0:T(8,128)(2,1)} %k_ref.1, bf16[64,1024]{1,0:T(8,128)(2,1)} %v_ref.1, ...), custom_call_target="tpu_custom_call" | custom-call | flops 1500000000 | bytes 2000000 | tf_op jit(solution)/shard_map/pallas_call | solution.py:420
  28.4 0.8 %shard_map.102 = (bf16[64,1024]{1,0:T(8,128)(2,1)}, bf16[64,1024]{1,0:T(8,128)(2,1)}, bf16[64,1024]{1,0:T(8,128)(2,1)}, bf16[64,1024]{1,0:T(8,128)(2,1)}, bf16[8,64]{1,0:T(8,128)(2,1)}) custom-call(bf16[128,1024]{1,0:T(8,128)(2,1)S(1)} %get-tuple-element.13.first, bf16[144,1024]{1,0:T(8,128)(2,1)S(1)} %get-tuple-element.14.second, ...), custom_call_target="tpu_custom_call" | custom-call | bytes 1000000 | tf_op jit(solution)/shard_map/pallas_call | solution.py:438
